TPU v7x, 128 devices: a whole 4x4x4 slice. The times are simulated.
128 devices in a mesh: noise: 8 (over y, core), dp: 16 (over x, z).
Axes of the slice: x: 4, y: 4, z: 4, core: 2. Of those that a mesh axis runs over, the one named last changes fastest.
Arguments:
- noise_latents: bfloat16 [16384, 2048], P('noise', 'dp')
- data_latents: bfloat16 [16384, 2048], P('dp', 'noise')
Outputs:
- targets: float32 [16384, 2048], P('noise', 'dp')
- potential_rows: float32 [16384], P('noise')
- potential_cols: float32 [16384], P('dp')
All inputs are finite; a program needn't handle non-finite values.
Results may differ from a plain program's by a relative error of at most 0.0023.
Values may be sent and summed in bfloat16 or wider, within the bound.
A program may use at most 128 MiB of HBM per device.

v0:
```python
import functools
import math

import jax
import jax.numpy as jnp
from jax import lax
from jax.experimental import pallas as pl
from jax.experimental.pallas import tpu as pltpu
from jax.sharding import PartitionSpec as P

ITERS = 3
EPSILON = 0.04
LOG2E = 1.0 / math.log(2.0)
MESH = pl.DeviceIdType.MESH
LANES = 128
TILE = 32
SIDE = 4
STRIPS = 4


def wrap(index, size):
    return lax.rem(index, size)


def spread_lanes(ref, row):
    return jnp.broadcast_to(ref[pl.ds(row, 1), :], (LANES, LANES)).T


def exchange(buf, send, recv, step, parts, me, size, peer_id, started):
    for k in range(1, size):
        pltpu.make_async_remote_copy(
            src_ref=buf.at[step, me, pl.ds(0, parts)],
            dst_ref=buf.at[step, me, pl.ds(0, parts)],
            send_sem=send.at[step],
            recv_sem=recv.at[step],
            device_id=peer_id(wrap(me + k, size)),
            device_id_type=MESH,
        ).start()
    slots = buf.at[step, pl.ds(0, size - 1), pl.ds(0, parts)]
    every = pltpu.make_async_remote_copy(
        src_ref=slots,
        dst_ref=slots,
        send_sem=send.at[step],
        recv_sem=recv.at[step],
        device_id=peer_id(wrap(me + 1, size)),
        device_id_type=MESH,
    )
    every.wait_recv()
    started.append(every)


def combine(buf, step, size):
    top = buf[step, 0, 0]
    for s in range(1, size):
        top = jnp.maximum(top, buf[step, s, 0])
    total = buf[step, 0, 1] * jnp.exp2(buf[step, 0, 0] - top)
    for s in range(1, size):
        total = total + buf[step, s, 1] * jnp.exp2(buf[step, s, 0] - top)
    return top, total


def add_slots(buf, step, size):
    total = buf[step, 0, 0]
    for s in range(1, size):
        total = total + buf[step, s, 0]
    return total


def kernel(
    rsize, csize, width,
    noise_ref, data_ref,
    targets, rows_out, cols_out,
    noise_all, data_all, scores, weights,
    shift, first, scale, part, data_part, colvec, rowpack, colpack, sqx, sqy, swap,
    col_buf, row_buf, out_buf, own_buf, far_buf, near_buf, in_sum,
    col_send, col_recv, row_send, row_recv, swap_send, swap_recv,
    cross_send, cross_recv, noise_send, noise_recv, data_send, data_recv,
    sum_send, sum_recv, in_send, in_recv, keep,
):
    rows, cols = scores.shape
    n = lax.axis_index("noise")
    d = lax.axis_index("dp")
    x, z = d // SIDE, lax.rem(d, SIDE)
    y, core = n // 2, lax.rem(n, 2)
    kind = lax.rem((x + 1) // 2, 2)
    pair = x // 2
    side = lax.rem(x, 2)
    home = core == kind
    kappa = LOG2E / EPSILON
    log_rows = math.log2(rows * csize)
    log_cols = math.log2(cols * rsize)
    chunks = cols // LANES
    row_blocks = rows // LANES
    tiles = rows // TILE
    started = []

    def around(value):
        return lax.rem(value + SIDE, SIDE)

    def device(xi, yi, zi, ci):
        return (yi * 2 + ci, xi * SIDE + zi)

    def x_at(which, of_kind):
        return which * (3 - 2 * of_kind) + of_kind

    me_row = pair * SIDE + z
    me_col = y * 4 + kind * 2 + core

    def row_peer(p):
        return device(x_at(p // SIDE, kind), y, lax.rem(p, SIDE), core)

    def col_peer(p):
        return device(x_at(pair, lax.rem(p // 2, 2)), p // 4, z, lax.rem(p, 2))

    sibling = device(x, y, z, 1 - core)
    partner = x + 1 - 2 * side
    mate = SIDE - 1 - x
    opposite = around(x + 2)

    barrier = pltpu.get_barrier_semaphore()
    greeted = [row_peer(wrap(me_row + k, rsize)) for k in range(1, rsize)]
    greeted += [col_peer(wrap(me_col + k, csize)) for k in range(1, csize)]
    greeted += [device(opposite, y, z, 0), device(opposite, y, z, 1), device(mate, y, z, 1 - core)]
    for to in greeted:
        pl.semaphore_signal(barrier, inc=1, device_id=to, device_id_type=MESH)
    pl.semaphore_wait(barrier, len(greeted))

    def remote(src, dst, send, recv, to):
        return pltpu.make_async_remote_copy(
            src_ref=src, dst_ref=dst, send_sem=send, recv_sem=recv, device_id=to, device_id_type=MESH
        )

    def begin(copy):
        copy.start()
        started.append(copy)

    def lane(c):
        return slice(LANES * c, LANES * (c + 1))

    HOP = (1, -1)
    ORDER = (0, 1, 3, 2)
    own = x * SIDE + z

    def cross_copy(i, half, to):
        return remote(
            noise_ref.at[pl.ds(half * rows, rows)], noise_all.at[own], cross_send.at[i], cross_recv.at[x], to
        )

    def cross_wait(xi):
        remote(
            noise_ref.at[pl.ds(0, rows)], noise_all.at[xi * SIDE + z], cross_send.at[0], cross_recv.at[xi], sibling
        ).wait_recv()

    there = jnp.where(home, mate, opposite)
    back = jnp.where(home, x, partner)
    last = cross_copy(3, core, device(partner, y, z, core))

    def noise_copy(xi, t, forward, slot):
        at = pl.ds(t * (rows // 2), rows // 2) if forward else pl.ds(0, rows)
        f = int(forward)
        return remote(
            noise_all.at[slot, at], noise_all.at[slot, at],
            noise_send.at[xi, t, f], noise_recv.at[xi, t, f], device(x, y, around(z + HOP[t]), core),
        )

    def noise_wait(xi, t, forward):
        slot = xi * SIDE + around(z - HOP[t] * (2 if forward else 1))
        noise_copy(xi, t, forward, slot).wait_recv()
        return slot

    def data_copy(r, index, where, lo, size, to, own=False):
        at = pl.ds(lo, size)
        block = side if r == 0 else 1 - side
        dst = data_all.at[block, where, at]
        return remote(data_ref.at[at] if own else dst, dst, data_send.at[r, index], data_recv.at[r, index], to)

    half_cols = cols // 4
    full_cols = cols // 2

    def along_y(step, c):
        return around(y + step) * 2 + c

    def data_wait(r, index, where, lo, size):
        data_copy(r, index, where, lo, size, sibling).wait_recv()

    for t in (0, 1):
        begin(data_copy(0, t, n, 0, full_cols, device(x, around(y + HOP[t]), z, core), own=True))
    begin(remote(
        data_ref.at[pl.ds(0, full_cols)], data_all.at[side, n],
        data_send.at[1, 9], data_recv.at[1, 9], device(partner, y, z, core),
    ))
    begin(cross_copy(2, 1 - core, device(back, y, z, 1 - core)))

    @pl.when(home)
    def _():
        noise_all[own] = noise_ref[pl.ds(pl.multiple_of(core * rows, rows), rows), :]

    @pl.when(jnp.logical_not(home))
    def _():
        last.start()

    begin(cross_copy(0, 0, device(there, y, z, 0)))
    begin(cross_copy(1, 1, device(there, y, z, 1)))
    begin(data_copy(0, 4, n, 0, full_cols, sibling, own=True))

    data_all[side, n] = data_ref[...]

    @pl.when(jnp.logical_not(home))
    def _():
        cross_wait(x)

    for t in (0, 1):
        begin(noise_copy(x, t, False, own))
    scores[...] = jnp.zeros_like(scores)
    part[...] = jnp.zeros_like(part)
    data_part[...] = jnp.zeros_like(data_part)
    data_wait(1, 9, n, 0, full_cols)
    for t in (0, 1):
        begin(data_copy(1, t, n, 0, full_cols, device(x, around(y + HOP[t]), z, core)))
    begin(data_copy(1, 4, n, 0, full_cols, sibling))
    for xi in (partner, mate, opposite):
        cross_wait(xi)
        for t in (0, 1):
            begin(noise_copy(xi, t, False, xi * SIDE + z))
    for r in (0, 1):
        for t in (0, 1):
            where = along_y(-HOP[t], core)
            data_wait(r, t, where, 0, full_cols)
            begin(data_copy(r, 2 + t, where, t * half_cols, half_cols, device(x, around(y + HOP[t]), z, core)))
            begin(data_copy(r, 5 + t, where, 0, full_cols, sibling))
    by_data = [around(y + step) for step in ORDER]
    for xi in by_data:
        for t in (0, 1):
            begin(noise_copy(xi, t, True, noise_wait(xi, t, False)))
    for r in (0, 1):
        data_wait(r, 4, along_y(0, 1 - core), 0, full_cols)
        for t in (0, 1):
            data_wait(r, 5 + t, along_y(-HOP[t], 1 - core), 0, full_cols)

    def squares(block):
        value = block.astype(jnp.float32)
        return value * value

    def chunk_product(q, m):
        both = jnp.concatenate([noise_all[2 * q], noise_all[2 * q + 1]], axis=1)
        cut = pl.ds(pl.multiple_of(m * 256, 256), 256)
        piece = data_all[m // 4, q, pl.ds(pl.multiple_of(lax.rem(m, 4) * 256, 256), 256), :]
        data_part[cut, :] += squares(piece[:, :LANES]) + squares(piece[:, LANES:])
        return lax.dot_general(both, piece, (((1,), (1,)), ((), ())), preferred_element_type=jnp.float32)

    def norms(q):
        def norm(r, carry):
            cut = pl.ds(pl.multiple_of(r * 64, 64), 64)
            part[cut, :] += squares(noise_all[2 * q, cut, :]) + squares(noise_all[2 * q + 1, cut, :])
            return carry

        lax.fori_loop(0, rows // 64, norm, 0)

    def chunk(q):
        def column(m, carry):
            cut = pl.ds(pl.multiple_of(m * 256, 256), 256)
            scores[:, cut] += chunk_product(q, m)
            return carry

        lax.fori_loop(0, cols // 256, column, 0)
        norms(q)

    mine = z // 2

    def early(i, carry):
        chunk(around(y + i + i // 2) * 2 + mine)
        return carry

    lax.fori_loop(0, 3, early, 0)

    def late(xi):
        for t in (0, 1):
            noise_wait(xi, t, True)
        chunk(xi * 2 + 1 - mine)

    late(by_data[0])
    for r in (0, 1):
        for t in (0, 1):
            where = along_y(2, core)
            data_wait(r, 2 + t, where, t * half_cols, half_cols)
            begin(data_copy(r, 7 + t, where, t * half_cols, half_cols, sibling))
        if r == 0:
            late(by_data[1])
            late(by_data[2])
    for r in (0, 1):
        for t in (0, 1):
            data_wait(r, 7 + t, along_y(2, 1 - core), t * half_cols, half_cols)
    for t in (0, 1):
        noise_wait(by_data[3], t, True)

    factor = 2.0 * kappa / width
    q_mine, q_other = around(y + 2) * 2 + mine, around(y + 2) * 2 + 1 - mine
    for q in (q_mine, q_other):
        norms(q)

    def row_shift(r, carry):
        at = pl.ds(pl.multiple_of(r * 128, 128), 128)
        total = jnp.sum(part[at, :], axis=1, keepdims=True) * (-kappa / width)
        shift[at, :] = jnp.broadcast_to(total, (128, LANES))
        return carry

    lax.fori_loop(0, rows // 128, row_shift, 0)

    def final(m, carry):
        cut = pl.ds(pl.multiple_of(m * 256, 256), 256)
        value = scores[:, cut]
        for q in (q_mine, q_other):
            value = value + chunk_product(q, m)
        value = value * factor
        scores[:, cut] = value
        for e in (0, 1):
            top = jnp.max(value[:, LANES * e:LANES * (e + 1)] + shift[...], axis=0, keepdims=True)
            col_buf[0, me_col, 0, pl.ds(2 * m + e, 1), :] = top
            colvec[:, pl.ds(pl.multiple_of(m * 256 + e * LANES, LANES), LANES)] = jnp.broadcast_to(top, (8, LANES))
        return carry

    lax.fori_loop(0, cols // 256, final, 0)

    def fold(block, op):
        out = block[0:8]
        for r in range(1, TILE // 8):
            out = op(out, block[8 * r:8 * r + 8])
        return out

    def spread_cols():
        for c in range(chunks):
            colvec[:, lane(c)] = jnp.broadcast_to(colpack[pl.ds(c, 1), :], (8, LANES))

    def tall(ref, c):
        return jnp.concatenate([ref[:, lane(c)]] * (TILE // 8), axis=0)

    def tile_at(t):
        return pl.ds(pl.multiple_of(t * TILE, TILE), TILE)

    def loop(body, init):
        return lax.fori_loop(0, tiles, body, init, unroll=2)

    zeros = tuple(jnp.zeros((8, LANES), jnp.float32) for _ in range(chunks))

    def exp_step(t, accs):
        at = tile_at(t)
        add = shift[at, :]
        return tuple(
            accs[c] + fold(jnp.exp2(scores[at, lane(c)] + add - tall(colvec, c)), jnp.add)
            for c in range(chunks)
        )

    sums = loop(exp_step, zeros)
    for c in range(chunks):
        col_buf[0, me_col, 1, pl.ds(c, 1), :] = jnp.sum(sums[c], axis=0, keepdims=True)
    exchange(col_buf, col_send, col_recv, 0, 2, me_col, csize, col_peer, started)
    top, total = combine(col_buf, 0, csize)
    col_pot = -log_cols - top - jnp.log(total) * LOG2E
    colpack[...] = col_pot
    spread_cols()

    def row_step(t, carry):
        at = tile_at(t)
        top = scores[at, lane(0)] + tall(colvec, 0)
        for c in range(1, chunks):
            top = jnp.maximum(top, scores[at, lane(c)] + tall(colvec, c))
        first[at, :] = top
        total = None
        for c in range(chunks):
            value = jnp.exp2(scores[at, lane(c)] + tall(colvec, c) - top)
            scores[at, lane(c)] = value
            total = value if total is None else total + value
        part[at, :] = total
        return carry

    loop(row_step, 0)
    for b in range(row_blocks):
        at = pl.ds(b * LANES, LANES)
        tops = first[at, :].T
        top = jnp.max(tops, axis=0, keepdims=True)
        row_buf[0, me_row, 0, pl.ds(b, 1), :] = top
        row_buf[0, me_row, 1, pl.ds(b, 1), :] = jnp.sum(part[at, :].T * jnp.exp2(tops - top), axis=0, keepdims=True)
    exchange(row_buf, row_send, row_recv, 0, 2, me_row, rsize, row_peer, started)
    top, total = combine(row_buf, 0, rsize)
    row_lse = top + jnp.log(total) * LOG2E
    rowpack[...] = row_lse
    for b in range(row_blocks):
        at = pl.ds(b * LANES, LANES)
        base = jnp.exp2(first[at, :] - spread_lanes(rowpack, b))
        first[at, :] = base
        scale[at, :] = base

    def col_step(t, accs):
        at = tile_at(t)
        mul = scale[at, :]
        return tuple(accs[c] + fold(scores[at, lane(c)] * mul, jnp.add) for c in range(chunks))

    def sum_step(keep_values):
        def body(t, carry):
            at = tile_at(t)
            total = None
            for c in range(chunks):
                value = scores[at, lane(c)] * tall(colvec, c)
                if keep_values:
                    scores[at, lane(c)] = value
                total = value if total is None else total + value
            part[at, :] = total * first[at, :]
            return carry

        return body

    for step in range(1, ITERS):
        sums = loop(col_step, zeros)
        for c in range(chunks):
            col_buf[step, me_col, 0, pl.ds(c, 1), :] = jnp.sum(sums[c], axis=0, keepdims=True)
        exchange(col_buf, col_send, col_recv, step, 1, me_col, csize, col_peer, started)
        ratio = 1.0 / add_slots(col_buf, step, csize)
        colpack[...] = ratio
        spread_cols()
        loop(sum_step(step == ITERS - 1), 0)
        for b in range(row_blocks):
            at = pl.ds(b * LANES, LANES)
            row_buf[step, me_row, 0, pl.ds(b, 1), :] = jnp.sum(part[at, :].T, axis=0, keepdims=True)
        exchange(row_buf, row_send, row_recv, step, 1, me_row, rsize, row_peer, started)
        total = add_slots(row_buf, step, rsize)
        rowpack[...] = 1.0 / total
        for b in range(row_blocks):
            at = pl.ds(b * LANES, LANES)
            scale[at, :] = first[at, :] * spread_lanes(rowpack, b)

    def weigh(r):
        def body(t, carry):
            at = pl.ds(pl.multiple_of(r * (rows // 2) + t * TILE, TILE), TILE)
            mul = scale[at, :]
            for c in range(chunks):
                weights[at, lane(c)] = (scores[at, lane(c)] * mul).astype(jnp.bfloat16)
            return carry

        lax.fori_loop(0, tiles // 2, body, 0, unroll=2)

    def swap_copy(i, to):
        return remote(swap.at[0], swap.at[i], swap_send.at[i], swap_recv.at[i], to)

    def potentials():
        for c in range(chunks):
            sqy[pl.ds(c, 1), :] = jnp.sum(data_part[pl.ds(c * LANES, LANES), :].T, axis=0, keepdims=True)
        cols_pot = (col_pot + jnp.log(ratio) * LOG2E + (log_rows - log_cols)) / kappa + sqy[...] / width
        colpack[...] = cols_pot
        cols_out[...] = colpack[pl.ds(pl.multiple_of(side * 8, 8), 8), :]
        for b in range(row_blocks):
            sqx[pl.ds(b, 1), :] = shift[pl.ds(b * LANES, LANES), :].T[0:1]
        swap[0] = -(log_rows + row_lse + jnp.log(total) * LOG2E + sqx[...]) / kappa
        begin(swap_copy(1, sibling))
        for i in (0, 1):
            begin(remote(
                swap.at[0], swap.at[2 + core], swap_send.at[2 + i], swap_recv.at[2 + core], device(partner, y, z, i)
            ))

    strip = rows // 2

    def strip_rows(s):
        return pl.ds(pl.multiple_of(lax.rem(s, 2) * strip, strip), strip)

    def strip_blocks(s):
        begins = s < 2
        return jnp.where(begins, opposite, mate), jnp.where(begins, partner, x)

    def product(s, to_z):
        cut = pl.ds(pl.multiple_of(lax.rem(to_z, 2) * LANES, LANES), LANES)
        total = None
        for k in (0, 1):
            block = jnp.concatenate(
                [data_all[k, xi * 2 + to_z // 2, :, cut] for xi in strip_blocks(s)], axis=1
            )
            value = jnp.dot(
                weights[strip_rows(s), k * full_cols:(k + 1) * full_cols], block,
                preferred_element_type=jnp.float32,
            )
            total = value if total is None else total + value
        return total

    def sum_copy(s, t, index, src, dst):
        to = device(x, y, around(z + HOP[t]), core)
        return remote(src, dst, sum_send.at[s, t, index], sum_recv.at[s, t, index], to)

    def far_copy(s, t):
        return sum_copy(s, t, 0, out_buf.at[s, 2, t], far_buf.at[s, t])

    def direct_copy(s, t):
        return sum_copy(s, t, 1, out_buf.at[s, t, 1 - t], near_buf.at[s, t, 1 - t])

    def added_copy(s, t):
        return sum_copy(s, t, 2, out_buf.at[s, t, t], near_buf.at[s, t, t])

    def in_copy(s, e, g, a, to):
        r = lax.rem(s, 2)
        return remote(
            own_buf.at[s, e], in_sum.at[g, a, strip_rows(s)], in_send.at[s, e], in_recv.at[r, g, a], to
        )

    def out_copy(s, e):
        return in_copy(s, e, 1 - e, core, device(strip_blocks(s)[e], y, z, kind))

    def add_strip(s):
        for t in (0, 1):
            direct_copy(s, t).wait_recv()
            added_copy(s, t).wait_recv()
        for e in (0, 1):
            own_buf[s, e] = (
                own_buf[s, e] + near_buf[s, 0, e].astype(jnp.float32) + near_buf[s, 1, e].astype(jnp.float32)
            )
            if e == 0:
                out_copy(s, 0).start()
        stays = jnp.logical_and(home, s >= 2)

        @pl.when(stays)
        def _():
            in_sum[0, core, strip_rows(s), :] = own_buf[s, 1]

        @pl.when(jnp.logical_not(stays))
        def _():
            out_copy(s, 1).start()

    def send_strip(s, carry):
        @pl.when(s < 2)
        def _():
            weigh(s)

        value = product(s, around(z + 2))
        for t in (0, 1):
            out_buf[s, 2, t] = value[:, lane(t)].astype(jnp.bfloat16)
            far_copy(s, t).start()
        for t in (0, 1):
            value = product(s, around(z + HOP[t]))
            out_buf[s, t, 1 - t] = value[:, lane(1 - t)].astype(jnp.bfloat16)
            direct_copy(s, t).start()
            keep[t] = value[:, lane(t)]
        value = product(s, z)
        for e in (0, 1):
            own_buf[s, e] = value[:, lane(e)]
        for t in (0, 1):
            far_copy(s, t).wait_recv()
            out_buf[s, t, t] = (keep[t] + far_buf[s, t].astype(jnp.float32)).astype(jnp.bfloat16)
            added_copy(s, t).start()

        @pl.when(s > 0)
        def _():
            add_strip(jnp.maximum(s - 1, 0))

        return carry

    lax.fori_loop(0, STRIPS, send_strip, 0)
    potentials()
    add_strip(STRIPS - 1)

    swap_copy(1, sibling).wait_recv()
    for i in (0, 1):
        remote(swap.at[0], swap.at[2 + i], swap_send.at[2 + i], swap_recv.at[2 + i], sibling).wait_recv()
    half = rows // LANES
    for a in (0, 1):
        mine_row = jnp.where(core == a, swap[0], swap[1])
        rows_out[pl.ds(a * half, half), :] = jnp.where(home, mine_row, swap[2 + a])

    def wait_in(r, g, a):
        in_copy(r, 0, g, a, sibling).wait_recv()

    for r in (0, 1):
        wait_in(r, 1, 0)
        wait_in(r, 1, 1)
        wait_in(r, 0, 1 - core)

        @pl.when(jnp.logical_not(home))
        def _():
            wait_in(r, 0, core)

        for a in (0, 1):
            at = pl.ds(r * strip, strip)
            targets[pl.ds(a * rows + r * strip, strip), :] = in_sum[0, a, at, :] + in_sum[1, a, at, :]

    def settle(s, carry):
        for t in (0, 1):
            far_copy(s, t).wait_send()
            direct_copy(s, t).wait_send()
            added_copy(s, t).wait_send()
        out_copy(s, 0).wait_send()

        @pl.when(jnp.logical_not(jnp.logical_and(home, s >= 2)))
        def _():
            out_copy(s, 1).wait_send()

        return carry

    lax.fori_loop(0, STRIPS, settle, 0)
    for copy in started:
        copy.wait_send()

    @pl.when(jnp.logical_not(home))
    def _():
        last.wait_send()


def shards(noise_latents, data_latents):
    nsize = lax.axis_size("noise")
    dsize = lax.axis_size("dp")
    block, piece = noise_latents.shape
    rows, cols = block // 2, 2 * data_latents.shape[0]
    rsize, csize = dsize // 2, nsize * 2
    vmem = pl.BlockSpec(memory_space=pltpu.VMEM)
    f32, bf16 = jnp.float32, jnp.bfloat16
    strip = rows // 2
    row_vec, col_vec = (rows // LANES, LANES), (cols // LANES, LANES)
    sems = pltpu.SemaphoreType.DMA
    targets, rows_pot, cols_pot = pl.pallas_call(
        functools.partial(kernel, rsize, csize, piece * dsize),
        out_shape=(
            jax.ShapeDtypeStruct((block, piece), f32),
            jax.ShapeDtypeStruct((block // LANES, LANES), f32),
            jax.ShapeDtypeStruct((cols // 2 // LANES, LANES), f32),
        ),
        in_specs=[vmem] * 2,
        out_specs=(vmem,) * 3,
        scratch_shapes=[
            pltpu.VMEM((dsize, rows, piece), bf16),
            pltpu.VMEM((2, nsize) + data_latents.shape, bf16),
            pltpu.VMEM((rows, cols), f32),
            pltpu.VMEM((rows, cols), bf16),
            pltpu.VMEM((rows, LANES), f32),
            pltpu.VMEM((rows, LANES), f32),
            pltpu.VMEM((rows, LANES), f32),
            pltpu.VMEM((rows, LANES), f32),
            pltpu.VMEM((cols, LANES), f32),
            pltpu.VMEM((8, cols), f32),
            pltpu.VMEM(row_vec, f32),
            pltpu.VMEM(col_vec, f32),
            pltpu.VMEM(row_vec, f32),
            pltpu.VMEM(col_vec, f32),
            pltpu.VMEM((4,) + row_vec, f32),
            pltpu.VMEM((ITERS, csize, 2) + col_vec, f32),
            pltpu.VMEM((ITERS, rsize, 2) + row_vec, f32),
            pltpu.VMEM((STRIPS, 3, 2, strip, LANES), bf16),
            pltpu.VMEM((STRIPS, 2, strip, LANES), f32),
            pltpu.VMEM((STRIPS, 2, strip, LANES), bf16),
            pltpu.VMEM((STRIPS, 2, 2, strip, LANES), bf16),
            pltpu.VMEM((2, 2, rows, LANES), f32),
            sems((ITERS,)),
            sems((ITERS,)),
            sems((ITERS,)),
            sems((ITERS,)),
            sems((4,)),
            sems((4,)),
            sems((4,)),
            sems((4,)),
            sems((SIDE, 2, 2)),
            sems((SIDE, 2, 2)),
            sems((2, 10)),
            sems((2, 10)),
            sems((STRIPS, 2, 3)),
            sems((STRIPS, 2, 3)),
            sems((STRIPS, 2)),
            sems((2, 2, 2)),
            pltpu.VMEM((2, strip, LANES), f32),
        ],
        compiler_params=pltpu.CompilerParams(
            collective_id=0, has_side_effects=True, vmem_limit_bytes=60 * 2**20
        ),
    )(noise_latents, data_latents)
    return targets, rows_pot.reshape(block), cols_pot.reshape(cols // 2)


def solution(mesh):
    return jax.shard_map(
        shards,
        mesh=mesh,
        in_specs=(P("noise", "dp"), P("dp", "noise")),
        out_specs=(P("noise", "dp"), P("noise"), P("dp")),
        check_vma=False,
    )
```

profile of v0, /device:TPU:1, one launch (start us, length us, event | category | flops | bytes accessed | tf_op | source)
XLA Modules:
  0.0 153.8 jit_solution(14371034224036660583)
XLA Ops:
  0.6 149.7 %shard_map.49 = (f32[2048,128]{1,0:T(8,128)}, f32[16,128]{1,0:T(8,128)}, f32[8,128]{1,0:T(8,128)}) custom-call(bf16[2048,128]{1,0:T(8,128)(2,1)} %noise_ref.1, bf16[1024,256]{1,0:T(8,128)(2,1)} %data_ref.1), custom_call_target="tpu_custom_call" | custom-call | tf_op jit(solution)/shard_map/pallas_call | solution.py:613
  150.3 0.0 copy-start
  150.3 2.3 %copy.8 = f32[2048,128]{1,0:T(8,128)} copy(f32[2048,128]{1,0:T(8,128)} %get-tuple-element.12) | data formatting | bytes 2097152
  152.6 0.0 copy-done
  152.6 0.0 copy-start.1
  152.6 0.6 copy.9
  153.2 0.1 copy-done.1
  153.3 0.6 copy.10
Async XLA Ops:
  150.3 2.3 %copy-start = (f32[16,128]{1,0:T(8,128)S(1)}, f32[16,128]{1,0:T(8,128)}, u32[]{:S(2)}) copy-start(f32[16,128]{1,0:T(8,128)} %get-tuple-element.7) | copy-start | bytes 24580
  152.6 0.7 copy-start.1
where the time goes:
time: 157 us; the launch traced here: 154 us
  Pallas kernels  150 us (96%)
  local copies, waits for them, and re-layouts  3.54 us (2%)
    pallas_call x1, Pallas kernels, shards(): pl.pallas_call(functools.partial(kernel, rsize, csize, piece * dsize), ou...  150 us
    unnamed x7, local copies, waits for them, and re-layouts  3.54 us

commit v1 on v0

--- a/solution.py
+++ b/solution.py
@@ -151,9 +151,8 @@
             noise_ref.at[pl.ds(0, rows)], noise_all.at[xi * SIDE + z], cross_send.at[0], cross_recv.at[xi], sibling
         ).wait_recv()
 
-    there = jnp.where(home, mate, opposite)
-    back = jnp.where(home, x, partner)
-    last = cross_copy(3, core, device(partner, y, z, core))
+    there = jnp.where(home, mate, partner)
+    aside = cross_copy(2, 1 - core, sibling)
 
     def noise_copy(xi, t, forward, slot):
         at = pl.ds(t * (rows // 2), rows // 2) if forward else pl.ds(0, rows)
@@ -183,13 +182,35 @@
     def data_wait(r, index, where, lo, size):
         data_copy(r, index, where, lo, size, sibling).wait_recv()
 
+    HALF = 9
+
+    def cross_data(h, own=False):
+        at = pl.ds(h * half_cols, half_cols)
+        dst = data_all.at[side if own else 1 - side, n, at]
+        return remote(
+            data_ref.at[at], dst, data_send.at[1, 11 + h], data_recv.at[1, 11 + h], device(partner, y, z, core)
+        )
+
+    def partner_y(t, h, back=0):
+        where = around(y + back) * 2 + core
+        to = device(x, around(y + HOP[t]), z, core)
+        return t if h == 0 else HALF + t, where, h * half_cols, half_cols, to
+
+    def partner_wait(t, h):
+        data_copy(1, *partner_y(t, h, -HOP[t])).wait_recv()
+
+    begin(cross_copy(0, 0, device(there, y, z, 0)))
+    begin(cross_copy(1, 1, device(there, y, z, 1)))
+
+    @pl.when(home)
+    def _():
+        aside.start()
+
     for t in (0, 1):
         begin(data_copy(0, t, n, 0, full_cols, device(x, around(y + HOP[t]), z, core), own=True))
-    begin(remote(
-        data_ref.at[pl.ds(0, full_cols)], data_all.at[side, n],
-        data_send.at[1, 9], data_recv.at[1, 9], device(partner, y, z, core),
-    ))
-    begin(cross_copy(2, 1 - core, device(back, y, z, 1 - core)))
+    for h in (0, 1):
+        begin(cross_data(h, own=True))
+    begin(data_copy(0, 4, n, 0, full_cols, sibling, own=True))
 
     @pl.when(home)
     def _():
@@ -197,45 +218,41 @@
 
     @pl.when(jnp.logical_not(home))
     def _():
-        last.start()
-
-    begin(cross_copy(0, 0, device(there, y, z, 0)))
-    begin(cross_copy(1, 1, device(there, y, z, 1)))
-    begin(data_copy(0, 4, n, 0, full_cols, sibling, own=True))
-
+        cross_wait(x)
+
+    for t in (0, 1):
+        begin(noise_copy(x, t, False, own))
     data_all[side, n] = data_ref[...]
-
-    @pl.when(jnp.logical_not(home))
-    def _():
-        cross_wait(x)
-
-    for t in (0, 1):
-        begin(noise_copy(x, t, False, own))
     scores[...] = jnp.zeros_like(scores)
     part[...] = jnp.zeros_like(part)
     data_part[...] = jnp.zeros_like(data_part)
-    data_wait(1, 9, n, 0, full_cols)
-    for t in (0, 1):
-        begin(data_copy(1, t, n, 0, full_cols, device(x, around(y + HOP[t]), z, core)))
-    begin(data_copy(1, 4, n, 0, full_cols, sibling))
-    for xi in (partner, mate, opposite):
+    for xi in (mate, partner):
         cross_wait(xi)
         for t in (0, 1):
             begin(noise_copy(xi, t, False, xi * SIDE + z))
-    for r in (0, 1):
-        for t in (0, 1):
-            where = along_y(-HOP[t], core)
-            data_wait(r, t, where, 0, full_cols)
-            begin(data_copy(r, 2 + t, where, t * half_cols, half_cols, device(x, around(y + HOP[t]), z, core)))
-            begin(data_copy(r, 5 + t, where, 0, full_cols, sibling))
+    slot = partner * SIDE + z
+    begin(remote(
+        noise_all.at[slot], noise_all.at[slot], cross_send.at[3], cross_recv.at[partner], device(mate, y, z, core)
+    ))
+    cross_data(0).wait_recv()
+    for t in (0, 1):
+        begin(data_copy(1, *partner_y(t, 0)))
+    for t in (0, 1):
+        where = along_y(-HOP[t], core)
+        data_wait(0, t, where, 0, full_cols)
+        begin(data_copy(0, 2 + t, where, t * half_cols, half_cols, device(x, around(y + HOP[t]), z, core)))
+        begin(data_copy(0, 5 + t, where, 0, full_cols, sibling))
+    cross_data(1).wait_recv()
+    for t in (0, 1):
+        begin(data_copy(1, *partner_y(t, 1)))
+    begin(data_copy(1, 4, n, 0, full_cols, sibling))
+    cross_wait(opposite)
+    for t in (0, 1):
+        begin(noise_copy(opposite, t, False, opposite * SIDE + z))
     by_data = [around(y + step) for step in ORDER]
     for xi in by_data:
         for t in (0, 1):
             begin(noise_copy(xi, t, True, noise_wait(xi, t, False)))
-    for r in (0, 1):
-        data_wait(r, 4, along_y(0, 1 - core), 0, full_cols)
-        for t in (0, 1):
-            data_wait(r, 5 + t, along_y(-HOP[t], 1 - core), 0, full_cols)
 
     def squares(block):
         value = block.astype(jnp.float32)
@@ -256,47 +273,86 @@
 
         lax.fori_loop(0, rows // 64, norm, 0)
 
-    def chunk(q):
+    near, other_block = side * 4, 4 - side * 4
+
+    def unit(q, block):
         def column(m, carry):
-            cut = pl.ds(pl.multiple_of(m * 256, 256), 256)
-            scores[:, cut] += chunk_product(q, m)
+            cut = pl.ds(pl.multiple_of((block + m) * 256, 256), 256)
+            scores[:, cut] += chunk_product(q, block + m)
             return carry
 
-        lax.fori_loop(0, cols // 256, column, 0)
+        lax.fori_loop(0, 4, column, 0)
+
+    mine = z // 2
+
+    def own_unit(q):
+        unit(q, near)
         norms(q)
 
-    mine = z // 2
-
-    def early(i, carry):
-        chunk(around(y + i + i // 2) * 2 + mine)
-        return carry
-
-    lax.fori_loop(0, 3, early, 0)
-
-    def late(xi):
+    def forward_wait(xi):
         for t in (0, 1):
             noise_wait(xi, t, True)
-        chunk(xi * 2 + 1 - mine)
-
-    late(by_data[0])
-    for r in (0, 1):
-        for t in (0, 1):
-            where = along_y(2, core)
-            data_wait(r, 2 + t, where, t * half_cols, half_cols)
-            begin(data_copy(r, 7 + t, where, t * half_cols, half_cols, sibling))
-        if r == 0:
-            late(by_data[1])
-            late(by_data[2])
-    for r in (0, 1):
-        for t in (0, 1):
-            data_wait(r, 7 + t, along_y(2, 1 - core), t * half_cols, half_cols)
-    for t in (0, 1):
-        noise_wait(by_data[3], t, True)
+
+    data_wait(0, 4, along_y(0, 1 - core), 0, full_cols)
+    for t in (0, 1):
+        data_wait(0, 5 + t, along_y(-HOP[t], 1 - core), 0, full_cols)
+
+    def early(i, carry):
+        own_unit(around(y + i + i // 2) * 2 + mine)
+        return carry
+
+    lax.fori_loop(0, 3, early, 0)
+
+    def pass_on(t):
+        where = along_y(-HOP[t], core)
+        begin(data_copy(1, 2 + t, where, t * half_cols, half_cols, device(x, around(y + HOP[t]), z, core)))
+
+    partner_wait(0, 0)
+    pass_on(0)
+    partner_wait(1, 0)
+    for t in (0, 1):
+        where = along_y(2, core)
+        data_wait(0, 2 + t, where, t * half_cols, half_cols)
+        begin(data_copy(0, 7 + t, where, t * half_cols, half_cols, sibling))
+    forward_wait(by_data[0])
+    own_unit(y * 2 + 1 - mine)
+    data_wait(1, 4, along_y(0, 1 - core), 0, full_cols)
+
+    def partner_mid(i, carry):
+        unit(y * 2 + i, other_block)
+        return carry
+
+    lax.fori_loop(0, 2, partner_mid, 0)
+    for t in (0, 1):
+        data_wait(0, 7 + t, along_y(2, 1 - core), t * half_cols, half_cols)
+    own_unit(around(y + 2) * 2 + mine)
+    partner_wait(1, 1)
+    pass_on(1)
+    partner_wait(0, 1)
+    for t in (0, 1):
+        begin(data_copy(1, 5 + t, along_y(-HOP[t], core), 0, full_cols, sibling))
+    for xi in by_data[1:3]:
+        forward_wait(xi)
+        own_unit(xi * 2 + 1 - mine)
+    for t in (0, 1):
+        data_wait(1, 5 + t, along_y(-HOP[t], 1 - core), 0, full_cols)
+
+    def partner_late(i, carry):
+        unit(around(y + 1 + 2 * (i // 2)) * 2 + lax.rem(i, 2), other_block)
+        return carry
+
+    lax.fori_loop(0, 4, partner_late, 0)
+    for t in (0, 1):
+        where = along_y(2, core)
+        data_wait(1, 2 + t, where, t * half_cols, half_cols)
+        begin(data_copy(1, 7 + t, where, t * half_cols, half_cols, sibling))
+    forward_wait(by_data[3])
+    for t in (0, 1):
+        data_wait(1, 7 + t, along_y(2, 1 - core), t * half_cols, half_cols)
 
     factor = 2.0 * kappa / width
     q_mine, q_other = around(y + 2) * 2 + mine, around(y + 2) * 2 + 1 - mine
-    for q in (q_mine, q_other):
-        norms(q)
+    norms(q_other)
 
     def row_shift(r, carry):
         at = pl.ds(pl.multiple_of(r * 128, 128), 128)
@@ -306,20 +362,25 @@
 
     lax.fori_loop(0, rows // 128, row_shift, 0)
 
-    def final(m, carry):
-        cut = pl.ds(pl.multiple_of(m * 256, 256), 256)
-        value = scores[:, cut]
-        for q in (q_mine, q_other):
-            value = value + chunk_product(q, m)
-        value = value * factor
-        scores[:, cut] = value
-        for e in (0, 1):
-            top = jnp.max(value[:, LANES * e:LANES * (e + 1)] + shift[...], axis=0, keepdims=True)
-            col_buf[0, me_col, 0, pl.ds(2 * m + e, 1), :] = top
-            colvec[:, pl.ds(pl.multiple_of(m * 256 + e * LANES, LANES), LANES)] = jnp.broadcast_to(top, (8, LANES))
-        return carry
-
-    lax.fori_loop(0, cols // 256, final, 0)
+    def final(block, qs):
+        def column(i, carry):
+            m = block + i
+            cut = pl.ds(pl.multiple_of(m * 256, 256), 256)
+            value = scores[:, cut]
+            for q in qs:
+                value = value + chunk_product(q, m)
+            value = value * factor
+            scores[:, cut] = value
+            for e in (0, 1):
+                top = jnp.max(value[:, LANES * e:LANES * (e + 1)] + shift[...], axis=0, keepdims=True)
+                col_buf[0, me_col, 0, pl.ds(2 * m + e, 1), :] = top
+                colvec[:, pl.ds(pl.multiple_of(m * 256 + e * LANES, LANES), LANES)] = jnp.broadcast_to(top, (8, LANES))
+            return carry
+
+        lax.fori_loop(0, 4, column, 0)
+
+    final(near, (q_other,))
+    final(other_block, (q_mine, q_other))
 
     def fold(block, op):
         out = block[0:8]
@@ -594,9 +655,9 @@
     for copy in started:
         copy.wait_send()
 
-    @pl.when(jnp.logical_not(home))
+    @pl.when(home)
     def _():
-        last.wait_send()
+        aside.wait_send()
 
 
 def shards(noise_latents, data_latents):
@@ -652,8 +713,8 @@
             sems((4,)),
             sems((SIDE, 2, 2)),
             sems((SIDE, 2, 2)),
-            sems((2, 10)),
-            sems((2, 10)),
+            sems((2, 13)),
+            sems((2, 13)),
             sems((STRIPS, 2, 3)),
             sems((STRIPS, 2, 3)),
             sems((STRIPS, 2)),

time: 157 us -> 148 us (0.943)
  Pallas kernels: 150 us -> 141 us
    pallas_call x1, Pallas kernels: 150 us -> 141 us  [shards(): pl.pallas_call(functools.partial(kernel, rsize, csize, piece * dsize), ou...]
where the time goes in v1:
time: 148 us; the launch traced here: 145 us
  Pallas kernels  141 us (95%)
  local copies, waits for them, and re-layouts  3.54 us (2%)
    pallas_call x1, Pallas kernels, shards(): pl.pallas_call(functools.partial(kernel, rsize, csize, piece * dsize), ou...  141 us
    unnamed x7, local copies, waits for them, and re-layouts  3.54 us

profile of v1, /device:TPU:1, one launch (start us, length us, event | category | flops | bytes accessed | tf_op | source)
XLA Modules:
  0.0 144.9 jit_solution(11386968608121188146)
XLA Ops:
  0.6 140.7 %shard_map.49 = (f32[2048,128]{1,0:T(8,128)}, f32[16,128]{1,0:T(8,128)}, f32[8,128]{1,0:T(8,128)}) custom-call(bf16[2048,128]{1,0:T(8,128)(2,1)} %noise_ref.1, bf16[1024,256]{1,0:T(8,128)(2,1)} %data_ref.1), custom_call_target="tpu_custom_call" | custom-call | tf_op jit(solution)/shard_map/pallas_call | solution.py:674
  141.3 0.0 copy-start
  141.3 2.3 %copy.8 = f32[2048,128]{1,0:T(8,128)} copy(f32[2048,128]{1,0:T(8,128)} %get-tuple-element.12) | data formatting | bytes 2097152
  143.6 0.0 copy-done
  143.6 0.0 copy-start.1
  143.6 0.6 copy.9
  144.2 0.1 copy-done.1
  144.3 0.6 copy.10
Async XLA Ops:
  141.3 2.3 %copy-start = (f32[16,128]{1,0:T(8,128)S(1)}, f32[16,128]{1,0:T(8,128)}, u32[]{:S(2)}) copy-start(f32[16,128]{1,0:T(8,128)} %get-tuple-element.7) | copy-start | bytes 24580
  143.6 0.7 copy-start.1
